TPU v7x, 32 devices: a whole 2x2x4 slice. The times are simulated.
32 devices in a mesh: section: 2 (over y), dp: 16 (over z, x, core).
Axes of the slice: x: 2, y: 2, z: 4, core: 2. Of those that a mesh axis runs over, the one named last changes fastest.
Arguments:
- patches: bfloat16 [12544, 768], P('dp'), may hold values from -6 to 6
- captions: bfloat16 [8192, 768], P('dp'), may hold values from -6 to 6
- segments: int32 [64, 128], P('dp'), may hold values from 0 to 3, never falling along the last dimension, each value on 1 to 64 neighbouring positions
- seg_images: int32 [64, 4], P('dp'), may hold values from 0 to 1
- attn_w: bfloat16 [2, 768, 4608], P('section'), may hold values from -0.9 to 0.9
- w_in: bfloat16 [2, 768, 3072], P('section'), may hold values from -0.21875 to 0.21875
- w_out: bfloat16 [2, 3072, 768], P('section'), may hold values from -0.109375 to 0.109375
- norm_gains: float32 [2, 3, 768], P('section'), may hold values from 0.5 to 1.5
- cotangent: bfloat16 [8192, 768], P('dp'), may hold values from -6 to 6
Outputs:
- decoded: bfloat16 [8192, 768], P('dp', 'section')
- caption_grad: float32 [8192, 768], P('dp', 'section')
- patch_grad: float32 [12544, 768], P('dp', 'section')
- attn_grad: float32 [2, 768, 4608], P('section', 'dp')
- w_in_grad: float32 [2, 768, 3072], P('section', 'dp')
- w_out_grad: float32 [2, 3072, 768], P('section', 'dp')
- gain_grad: float32 [2, 3, 768], P('section', None, 'dp')
Inputs may be any that keep to these rules, and one draw needn't show every extreme that they name: Every caption row has its 4 segments in order, numbered from 0. seg_images[r, s] names one of the 2 images of the group of caption row r.
All inputs are finite; a program needn't handle non-finite values.
Results may differ from a plain program's by a relative error of at most 0.015.
Values may be sent and summed in bfloat16 or wider, within the bound.
A program may use at most 320 MiB of HBM per device.

v0:
```python
import functools
import jax
import jax.numpy as jnp
from jax import lax
from jax.experimental import pallas as pl
from jax.experimental.pallas import tpu as pltpu
from jax.sharding import PartitionSpec as P

D = 768
FF = 3072
HEADS = 12
HEAD = 64
PATCHES = 196
ROW = 128
SEGS = 4
MICRO = 2
IMG_MB = 2
ROWS_MB = 2
NORM_EPS = 1e-06
SCORE_SCALE = 0.125
MASKED = -1e30
ROOT_HALF = 0.7071067811865476
INV_ROOT_TWO_PI = 0.3989422804014327
MESH = pl.DeviceIdType.MESH
MIB = 1 << 20

LOW = jnp.bfloat16
WIDE = jnp.float32
IMG_ROWS = -(-PATCHES // 16) * 16
ENC_MB = IMG_MB * IMG_ROWS
ENC_ROWS = MICRO * ENC_MB
DEC_MB = ROWS_MB * ROW
DEC_ROWS = MICRO * DEC_MB
PAIR = 2 * HEAD
PAIRS = HEADS // 2
HALF = D // 2
QUARTER = D // 4
CROSS_PAIRS = 2
EXPAND_UNROLL = 1
BACK_UNROLL = 1
CONTEXT_UNROLL = 1
PROJECT_UNROLL = 1
BACK_PAIRS = 2
ROW_PAIRS = 3
SELF_PAIRS = 3
SELF_BACK_PAIRS = 3
DEEP = 256
SHALLOW = 384
CROSS_BACK_PAIRS = 2


def dot_nn(left, right):
    return lax.dot_general(left, right, (((1,), (0,)), ((), ())), preferred_element_type=WIDE)


def dot_nt(left, right):
    return lax.dot_general(left, right, (((1,), (1,)), ((), ())), preferred_element_type=WIDE)


def dot_tn(left, right):
    return lax.dot_general(left, right, (((0,), (0,)), ((), ())), preferred_element_type=WIDE)


def rows_at(start, size):
    return pl.ds(pl.multiple_of(start, 16), size)


def cols_at(start, size):
    if isinstance(start, int):
        return slice(start, start + size)
    return pl.ds(pl.multiple_of(start, 128), size)


def norm_hat(values):
    centred = values - jnp.mean(values, -1, keepdims=True)
    inverse = lax.rsqrt(jnp.mean(centred * centred, -1, keepdims=True) + NORM_EPS)
    return centred * inverse, inverse


def norm_low(values, gain):
    return (norm_hat(values)[0] * gain).astype(LOW)


def norm_back(upstream, values, gain):
    normed, inverse = norm_hat(values)
    scaled = upstream * gain
    inner = (
        scaled
        - jnp.mean(scaled, -1, keepdims=True)
        - normed * jnp.mean(scaled * normed, -1, keepdims=True)
    )
    return inner * inverse, jnp.sum(upstream * normed, 0, keepdims=True)


def gelu_parts(hidden):
    normal_cdf = 0.5 * (1.0 + lax.erf(hidden * ROOT_HALF))
    slope = normal_cdf + hidden * INV_ROOT_TWO_PI * jnp.exp(-0.5 * hidden * hidden)
    return hidden * normal_cdf, slope


def first_lanes(rows):
    return lax.broadcasted_iota(jnp.int32, (rows, PAIR), 1) < HEAD


def split_pair(block):
    first = (lax.broadcasted_iota(jnp.int32, (1, PAIR), 1) < HEAD).astype(WIDE)
    return jnp.concatenate([block * first.astype(LOW), block * (1.0 - first).astype(LOW)], 0)


def join_pair(stacked):
    rows = stacked.shape[0] // 2
    return jnp.where(first_lanes(rows), stacked[:rows], stacked[rows:])


def attend(pairs, bias):
    stacked = [split_pair(queries) * SCORE_SCALE for queries, _, _ in pairs]
    scores = [dot_nt(stack, pair[1]) + bias for stack, pair in zip(stacked, pairs)]
    powers = [jnp.exp(block - jnp.max(block, -1, keepdims=True)) for block in scores]
    scales = [1.0 / jnp.sum(block, -1, keepdims=True) for block in powers]
    return [
        join_pair(dot_nn(block.astype(LOW), pair[2]) * scale).astype(LOW)
        for block, pair, scale in zip(powers, pairs, scales)
    ]


def attend_back(pairs, bias):
    stacked = [split_pair(pair[0]) * SCORE_SCALE for pair in pairs]
    grads = [split_pair(pair[3]) for pair in pairs]
    scores = [dot_nt(pair[1], stack) + bias for pair, stack in zip(pairs, stacked)]
    grad_chances = [dot_nt(pair[2], grad) for pair, grad in zip(pairs, grads)]
    powers = [jnp.exp(block - jnp.max(block, 0, keepdims=True)) for block in scores]
    chances = [block * (1.0 / jnp.sum(block, 0, keepdims=True)) for block in powers]
    inner = [jnp.sum(left * right, 0, keepdims=True) for left, right in zip(grad_chances, chances)]
    grad_scores = [
        (chance * (grad - mean)).astype(LOW)
        for chance, grad, mean in zip(chances, grad_chances, inner)
    ]
    grad_keys = [dot_nn(grad, stack) for grad, stack in zip(grad_scores, stacked)]
    grad_values = [dot_nn(chance.astype(LOW), grad) for chance, grad in zip(chances, grads)]
    grad_queries = [
        join_pair(dot_tn(grad, pair[1])) * SCORE_SCALE for grad, pair in zip(grad_scores, pairs)
    ]
    return [
        tuple(part.astype(LOW) for part in parts)
        for parts in zip(grad_queries, grad_keys, grad_values)
    ]


def pair_cols(pair, column=0):
    start = column * D + pair * PAIR
    return cols_at(start, PAIR) if not isinstance(start, int) else slice(start, start + PAIR)


def tiles(width, body):
    loop(D // width, lambda j: body(cols_at(j * width, width), j * width))


def pair_group(step, size):
    first = (step % (PAIRS // size)) * size
    return [first + pair for pair in range(size)]


def attend_rows(qkv, rows, mixed, bias, group):
    pairs = [[qkv[rows, pair_cols(pair, part)] for part in range(3)] for pair in group]
    for pair, result in zip(group, attend(pairs, bias)):
        mixed[rows, pair_cols(pair)] = result


def attend_rows_back(qkv, rows, grad_mixed, grad_rows, bias, group):
    pairs = [
        [qkv[rows, pair_cols(pair, part)] for part in range(3)]
        + [grad_mixed[grad_rows, pair_cols(pair)]]
        for pair in group
    ]
    for pair, results in zip(group, attend_back(pairs, bias)):
        for part in range(3):
            qkv[rows, pair_cols(pair, part)] = results[part]


def loop(count, body, unroll=1):
    def several(i, carry):
        for k in range(unroll):
            body(i * unroll + k)
        return carry

    if count == unroll:
        several(0, 0)
    else:
        lax.fori_loop(0, count // unroll, several, 0)


def main_kernel(*refs):
    (
        patches, captions, segments, seg_images, attn_w, w_in, w_out, gains, cot,
        a_out, o_out, c_out, b_out, u_out, dqkv_out, g1_out, g2_out, dh_out,
        co_out, dq_out, up_out, dctx_out, gain_out, patch_own, decoded_own, caption_own, exch_out,
        wa, wi, wo, wctx, x, ct, a, o, b, c, qkv, u, slope, x1, x2, g1, g2, landed, dmix, ctx,
        co, cq, g2w, tmp, sent, bias, bias_t, exch, decoded_half,
        gain_rows, load_sem, out_sem, up_send, up_recv, ctx_send, ctx_recv,
    ) = refs
    section = lax.axis_index("section")
    dp = lax.axis_index("dp")
    quarter = dp % 4
    side = dp + 2 * (1 - 2 * ((dp // 2) % 2))
    twin = dp + 1 - 2 * (dp % 2)
    other_quarter = quarter + 2 * (1 - 2 * (quarter // 2))
    barrier = pltpu.get_barrier_semaphore()
    for target in ({"section": 1 - section}, {"dp": side}, {"dp": twin}):
        pl.semaphore_signal(barrier, inc=1, device_id=target, device_id_type=MESH)
    pl.semaphore_wait(barrier, 3)

    gain_out[...] = jnp.zeros_like(gain_out)

    def across(src, index):
        return pltpu.make_async_remote_copy(
            src_ref=src, dst_ref=landed.at[index], send_sem=up_send.at[index],
            recv_sem=up_recv.at[index], device_id={"section": 1 - section}, device_id_type=MESH)

    def ctx_part(index):
        return wctx.at[rows_at(index * QUARTER, QUARTER), :]

    def ctx_copy(src, part, target, slot):
        return pltpu.make_async_remote_copy(
            src_ref=src, dst_ref=ctx_part(part), send_sem=ctx_send.at[slot],
            recv_sem=ctx_recv.at[slot], device_id=target, device_id_type=MESH)

    def load(src, dst, slot):
        return pltpu.make_async_copy(src, dst, load_sem.at[slot])

    weight_loads = [
        load(attn_w.at[0, :, 0 : 3 * D], wa.at[:, 0 : 3 * D], 0),
        load(attn_w.at[0, :, 3 * D :], wa.at[:, 3 * D :], 1),
        load(w_in.at[0], wi, 2),
        load(w_out.at[0], wo, 3),
    ]

    gain_in = load(gains.at[0], gain_rows, 6)
    gain_in.start()

    def store(src, dst, slot):
        return pltpu.make_async_copy(src, dst, out_sem.at[slot])

    def add_gain(index, row):
        gain_out[index : index + 1, :] = gain_out[index : index + 1, :] + row

    def encoder():
        ctx_copy(
            attn_w.at[0, rows_at(quarter * QUARTER, QUARTER), 4 * D : 6 * D], quarter,
            {"section": 1 - section}, 0,
        ).start()
        rows_in = load(patches, g1.at[0 : patches.shape[0]], 4)
        rows_in.start()
        for copy in weight_loads:
            copy.start()
        rows_in.wait()
        for image in range(MICRO * IMG_MB):
            low_rows = g1[image * PATCHES : (image + 1) * PATCHES, :]
            x[image * IMG_ROWS : image * IMG_ROWS + PATCHES, :] = low_rows
            x[image * IMG_ROWS + PATCHES : (image + 1) * IMG_ROWS, :] = jnp.zeros(
                (IMG_ROWS - PATCHES, D), LOW
            )
        key_bias = jnp.where(
            lax.broadcasted_iota(jnp.int32, (1, IMG_ROWS), 1) < PATCHES, 0.0, MASKED
        )
        key_bias_t = jnp.where(
            lax.broadcasted_iota(jnp.int32, (IMG_ROWS, 1), 0) < PATCHES, 0.0, MASKED
        )

        def forward(micro):
            base = micro * ENC_MB
            rows = rows_at(base, ENC_MB)

            def low_norm(i):
                part = rows_at(base + i * IMG_ROWS, IMG_ROWS)
                a[part, :] = norm_low(x[part, :].astype(WIDE), first_gain)

            loop(IMG_MB, low_norm)

            @pl.when(micro == 0)
            def _():
                weight_loads[0].wait()

            def project(j):
                cols = cols_at(j * D, D)
                qkv[rows, cols] = dot_nn(a[rows, :], wa[:, cols]).astype(LOW)

            loop(3, project, PROJECT_UNROLL)

            def attend_image(i):
                image, group = i // (PAIRS // ROW_PAIRS), pair_group(i, ROW_PAIRS)
                attend_rows(qkv, rows_at(base + image * IMG_ROWS, IMG_ROWS), o, key_bias, group)

            loop(IMG_MB * PAIRS // ROW_PAIRS, attend_image)

            @pl.when(micro == 0)
            def _():
                weight_loads[1].wait()

            def tile(cols, start):
                mixed = dot_nn(o[rows, :], wa[:, cols_at(3 * D + start, SHALLOW)])
                x1[rows, cols] = x[rows, cols].astype(WIDE) + mixed

            tiles(SHALLOW, tile)

            def mid_norm(i):
                part = rows_at(base + i * IMG_ROWS, IMG_ROWS)
                b[part, :] = norm_low(x1[part, :], second_gain)

            loop(IMG_MB, mid_norm)

            @pl.when(micro == 0)
            def _():
                weight_loads[2].wait()

            @pl.when(micro > 0)
            def _():
                store(u.at[0:ENC_MB], u_out.at[rows], 3).wait()

            def expand(j):
                cols = cols_at(j * 512, 512)
                active, bend = gelu_parts(dot_nn(b[rows, :], wi[:, cols]))
                u[0:ENC_MB, cols] = active.astype(LOW)
                slope[rows, cols] = bend.astype(LOW)

            loop(FF // 512, expand, EXPAND_UNROLL)

            @pl.when(micro == 0)
            def _():
                weight_loads[3].wait()

            def tile(cols, start):
                x2[rows, cols] = x1[rows, cols] + dot_nn(u[0:ENC_MB, :], wo[:, cols])

            tiles(DEEP, tile)
            store(u.at[0:ENC_MB], u_out.at[rows], 3).start()

            def top_norm(i):
                part = rows_at(base + i * IMG_ROWS, IMG_ROWS)
                c[part, :] = norm_low(x2[part, :], third_gain)

            loop(IMG_MB, top_norm)
            across(c.at[rows, :], micro).start()

        loop(MICRO, forward)
        stores = [store(a, a_out, 0), store(o, o_out, 1), store(b, b_out, 2)]
        for copy in stores:
            copy.start()

        def backward(micro):
            base = micro * ENC_MB
            rows = rows_at(base, ENC_MB)
            across(c.at[rows, :], micro).wait()

            def top_norm(i):
                part = rows_at(base + i * IMG_ROWS, IMG_ROWS)
                upstream = landed[micro, rows_at(i * IMG_ROWS, IMG_ROWS), :].astype(WIDE)
                grad, gain_row = norm_back(upstream, x2[part, :], third_gain)
                x2[part, :] = grad
                g2[part, :] = grad.astype(LOW)
                add_gain(2, gain_row)

            loop(IMG_MB, top_norm)

            def expand(j):
                cols = cols_at(j * D, D)
                hidden = dot_nt(g2[rows, :], wo[cols, :])
                slope[rows, cols] = (hidden * slope[rows, cols].astype(WIDE)).astype(LOW)

            loop(FF // D, expand, BACK_UNROLL)
            store(slope.at[rows], dh_out.at[rows], 7).start()
            store(g2.at[rows], g2_out.at[rows], 6).start()
            def tile(cols, start):
                tmp[0:ENC_MB, cols] = dot_nt(slope[rows, :], wi[cols_at(start, DEEP), :])

            tiles(DEEP, tile)

            def mid_norm(i):
                part = rows_at(base + i * IMG_ROWS, IMG_ROWS)
                grad, gain_row = norm_back(
                    tmp[rows_at(i * IMG_ROWS, IMG_ROWS), :], x1[part, :], second_gain
                )
                grad = grad + x2[part, :]
                x1[part, :] = grad
                g1[part, :] = grad.astype(LOW)
                add_gain(1, gain_row)

            loop(IMG_MB, mid_norm)
            store(g1.at[rows], g1_out.at[rows], 5).start()
            def tile(cols, start):
                grads = dot_nt(g1[rows, :], wa[cols_at(start, SHALLOW), 3 * D : 4 * D])
                dmix[0:ENC_MB, cols] = grads.astype(LOW)

            tiles(SHALLOW, tile)

            def attend_image(i):
                image = i // (PAIRS // BACK_PAIRS)
                attend_rows_back(
                    qkv, rows_at(base + image * IMG_ROWS, IMG_ROWS), dmix,
                    rows_at(image * IMG_ROWS, IMG_ROWS), key_bias_t,
                    pair_group(i, BACK_PAIRS),
                )

            loop(IMG_MB * PAIRS // BACK_PAIRS, attend_image)
            def tile(cols, start):
                tmp[0:ENC_MB, cols] = dot_nt(qkv[rows, :], wa[cols_at(start, DEEP), 0 : 3 * D])

            tiles(DEEP, tile)

            def low_norm(i):
                part = rows_at(base + i * IMG_ROWS, IMG_ROWS)
                grad, gain_row = norm_back(
                    tmp[rows_at(i * IMG_ROWS, IMG_ROWS), :], x[part, :].astype(WIDE), first_gain
                )
                x1[part, :] = x1[part, :] + grad
                exch[part, :] = x1[part, HALF:].astype(LOW)
                add_gain(0, gain_row)

            loop(IMG_MB, low_norm)
            store(qkv.at[rows], dqkv_out.at[rows], 4).start()
            store(x1.at[rows, 0:HALF], patch_own.at[rows], 8).start()

        loop(MICRO, backward)
        store(exch, exch_out, 9).start()
        late = [
            store(qkv, dqkv_out, 4), store(g1, g1_out, 5), store(g2, g2_out, 6),
            store(slope, dh_out, 7), store(x1.at[:, 0:HALF], patch_own, 8), store(exch, exch_out, 9),
        ]
        for copy in stores + late + [store(u.at[0:ENC_MB], u_out.at[0:ENC_MB], 3)]:
            copy.wait()
        ctx_copy(
            attn_w.at[0, rows_at(quarter * QUARTER, QUARTER), 4 * D : 6 * D], quarter,
            {"section": 1 - section}, 0,
        ).wait_send()

    def decoder():
        rows_in = load(captions, x.at[0:DEC_ROWS], 4)
        cot_in = load(cot, ct, 5)
        rows_in.start()
        for copy in weight_loads:
            copy.start()
        cot_in.start()
        rows_in.wait()
        full = slice(0, DEC_ROWS)

        def low_norm(i):
            part = rows_at(i * ROW, ROW)
            a[part, :] = norm_low(x[part, :].astype(WIDE), first_gain)

        loop(DEC_ROWS // ROW, low_norm)
        weight_loads[0].wait()

        def project(j):
            cols = cols_at(j * D, D)
            qkv[full, cols] = dot_nn(a[full, :], wa[:, cols]).astype(LOW)

        loop(3, project)

        def segment_pair(row):
            across_rows = jnp.broadcast_to(
                segments[pl.ds(row, 1), :].astype(WIDE), (ROW, ROW)
            )
            return across_rows, across_rows.T

        def self_bias(row, transposed):
            along, down = segment_pair(row)
            sub = lax.broadcasted_iota(jnp.int32, (ROW, ROW), 0)
            lane = lax.broadcasted_iota(jnp.int32, (ROW, ROW), 1)
            order = (lane >= sub) if transposed else (sub >= lane)
            single = jnp.where((along == down) & order, 0.0, MASKED)
            return jnp.concatenate([single, single], 1 if transposed else 0)

        def self_attend(row):
            row_bias = self_bias(row, False)

            def some(i):
                attend_rows(qkv, rows_at(row * ROW, ROW), o, row_bias, pair_group(i, SELF_PAIRS))

            loop(PAIRS // SELF_PAIRS, some)

        loop(DEC_ROWS // ROW, self_attend)
        weight_loads[1].wait()
        def tile(cols, start):
            mixed = dot_nn(o[full, :], wa[:, cols_at(3 * D + start, SHALLOW)])
            x1[full, cols] = x[full, cols].astype(WIDE) + mixed

        tiles(SHALLOW, tile)

        def mid_norm(i):
            part = rows_at(i * ROW, ROW)
            c[part, :] = norm_low(x1[part, :], second_gain)

        loop(DEC_ROWS // ROW, mid_norm)
        def tile(cols, start):
            cq[:, cols] = dot_nn(c[full, :], wa[:, cols_at(4 * D + start, SHALLOW)]).astype(LOW)

        tiles(SHALLOW, tile)
        weight_loads[3].wait()
        cot_in.wait()

        def cot_project(j):
            cols = cols_at(j * D, D)
            slope[full, cols] = dot_nt(ct[...], wo[cols, :]).astype(LOW)

        loop(FF // D, cot_project)
        weight_loads[2].wait()

        ctx_copy(ctx_part(quarter), quarter, {"section": 1 - section}, 0).wait_recv()
        ctx_copy(ctx_part(quarter), quarter, {"dp": side}, 1).start()
        ctx_copy(ctx_part(quarter), quarter, {"dp": twin}, 2).start()
        ctx_copy(ctx_part(quarter), other_quarter, {"dp": side}, 1).wait_recv()
        ctx_copy(ctx_part(other_quarter), other_quarter, {"dp": twin}, 3).start()
        ctx_copy(ctx_part(quarter), quarter, {"dp": twin}, 2).wait_recv()
        ctx_copy(ctx_part(quarter), quarter, {"dp": twin}, 3).wait_recv()

        def cross_bias(micro):
            key = lax.broadcasted_iota(jnp.int32, (ROW, ENC_MB), 1)
            key_t = lax.broadcasted_iota(jnp.int32, (ENC_MB, ROW), 0)

            def one(i):
                row = micro * ROWS_MB + i
                along, down = segment_pair(row)
                image_along = jnp.zeros((ROW, ROW), WIDE)
                image_down = jnp.zeros((ROW, ROW), WIDE)
                for seg in range(SEGS):
                    image = seg_images[row, seg].astype(WIDE)
                    image_along = jnp.where(along == seg, image, image_along)
                    image_down = jnp.where(down == seg, image, image_down)
                allowed = jnp.zeros((ROW, ENC_MB), jnp.bool_)
                allowed_t = jnp.zeros((ENC_MB, ROW), jnp.bool_)
                for image in range(IMG_MB):
                    low, high = image * IMG_ROWS, image * IMG_ROWS + PATCHES
                    allowed = allowed | (
                        (key >= low) & (key < high) & (image_down[:, 0:1] == image)
                    )
                    allowed_t = allowed_t | (
                        (key_t >= low) & (key_t < high) & (image_along[0:1, :] == image)
                    )
                bias[rows_at(i * ROW, ROW), :] = jnp.where(allowed, 0.0, MASKED)
                bias_t[i] = jnp.where(allowed_t, 0.0, MASKED)

            loop(ROWS_MB, one)

        def cross(micro):
            cross_bias(micro)
            base = micro * DEC_MB
            rows = rows_at(base, DEC_MB)
            keys = rows_at(micro * ENC_MB, ENC_MB)
            across(sent.at[micro], micro).wait_recv()

            def context(j):
                cols = cols_at(j * D, D)
                ctx[keys, cols] = dot_nn(landed[micro], wctx[:, cols]).astype(LOW)

            loop(2, context, CONTEXT_UNROLL)

            def attend_some(i):
                half_bias = bias[...]
                group = [i * CROSS_PAIRS + k for k in range(CROSS_PAIRS)]
                pairs = [
                    (cq[rows, pair_cols(pair)], ctx[keys, pair_cols(pair)], ctx[keys, pair_cols(pair, 1)])
                    for pair in group
                ]
                results = attend(pairs, jnp.concatenate([half_bias, half_bias], 0))
                for pair, result in zip(group, results):
                    co[rows, pair_cols(pair)] = result

            loop(PAIRS // CROSS_PAIRS, attend_some)
            def tile(cols, start):
                mixed = dot_nn(co[rows, :], wa[:, cols_at(5 * D + start, SHALLOW)])
                x2[rows, cols] = x1[rows, cols] + mixed

            tiles(SHALLOW, tile)

            def top_norm(i):
                part = rows_at(base + i * ROW, ROW)
                b[part, :] = norm_low(x2[part, :], third_gain)

            loop(ROWS_MB, top_norm)

            def expand(j):
                cols = cols_at(j * 512, 512)
                active, bend = gelu_parts(dot_nn(b[rows, :], wi[:, cols]))
                u[rows, cols] = active.astype(LOW)
                slope[rows, cols] = (bend * slope[rows, cols].astype(WIDE)).astype(LOW)

            loop(FF // 512, expand, EXPAND_UNROLL)
            def tile(cols, start):
                tmp[0:DEC_MB, cols] = dot_nt(slope[rows, :], wi[cols_at(start, DEEP), :])

            tiles(DEEP, tile)

            def top_back(i):
                part = rows_at(base + i * ROW, ROW)
                grad, gain_row = norm_back(tmp[rows_at(i * ROW, ROW), :], x2[part, :], third_gain)
                grad = grad + ct[part, :].astype(WIDE)
                g2w[part, :] = grad
                g2[part, :] = grad.astype(LOW)
                add_gain(2, gain_row)

            loop(ROWS_MB, top_back)
            def tile(cols, start):
                grads = dot_nt(g2[rows, :], wa[cols_at(start, SHALLOW), 5 * D : 6 * D])
                dmix[0:DEC_MB, cols] = grads.astype(LOW)

            tiles(SHALLOW, tile)

            def attend_back_some(i):
                parts = [bias_t[j] for j in range(ROWS_MB)]
                group = [i * CROSS_BACK_PAIRS + k for k in range(CROSS_BACK_PAIRS)]
                pairs = [
                    (
                        cq[rows, pair_cols(pair)], ctx[keys, pair_cols(pair)],
                        ctx[keys, pair_cols(pair, 1)], dmix[0:DEC_MB, pair_cols(pair)],
                    )
                    for pair in group
                ]
                results = attend_back(pairs, jnp.concatenate(parts + parts, 1))
                for pair, grads in zip(group, results):
                    cq[rows, pair_cols(pair)] = grads[0]
                    ctx[keys, pair_cols(pair)] = grads[1]
                    ctx[keys, pair_cols(pair, 1)] = grads[2]

            loop(PAIRS // CROSS_BACK_PAIRS, attend_back_some)
            def tile(cols, start):
                sent[micro, :, cols] = dot_nt(ctx[keys, :], wctx[cols_at(start, DEEP), :]).astype(LOW)

            tiles(DEEP, tile)
            across(sent.at[micro], micro).start()

        loop(MICRO, cross)
        stores = [
            store(a.at[full], a_out.at[full], 0), store(o.at[full], o_out.at[full], 1),
            store(b.at[full], b_out.at[full], 2), store(u.at[full], u_out.at[full], 3),
            store(slope.at[full], dh_out.at[full], 7), store(g2.at[full], g2_out.at[full], 6),
            store(co, co_out, 10), store(cq, dq_out, 11), store(landed, up_out, 12),
            store(ctx, dctx_out, 13), store(c.at[full], c_out.at[full], 14),
        ]
        for copy in stores:
            copy.start()

        def finish(micro):
            base = micro * DEC_MB
            rows = rows_at(base, DEC_MB)
            def tile(cols, start):
                tmp[0:DEC_MB, cols] = dot_nt(cq[rows, :], wa[cols_at(start, SHALLOW), 4 * D : 5 * D])

            tiles(SHALLOW, tile)

            def mid_back(i):
                part = rows_at(base + i * ROW, ROW)
                grad, gain_row = norm_back(tmp[rows_at(i * ROW, ROW), :], x1[part, :], second_gain)
                grad = grad + g2w[part, :]
                x1[part, :] = grad
                g1[part, :] = grad.astype(LOW)
                add_gain(1, gain_row)

            loop(ROWS_MB, mid_back)
            def tile(cols, start):
                grads = dot_nt(g1[rows, :], wa[cols_at(start, SHALLOW), 3 * D : 4 * D])
                dmix[0:DEC_MB, cols] = grads.astype(LOW)

            tiles(SHALLOW, tile)

            def self_back(i):
                row_bias = self_bias(micro * ROWS_MB + i, True)

                def some(j):
                    attend_rows_back(
                        qkv, rows_at(base + i * ROW, ROW), dmix, rows_at(i * ROW, ROW), row_bias,
                        pair_group(j, SELF_BACK_PAIRS),
                    )

                loop(PAIRS // SELF_BACK_PAIRS, some)

            loop(ROWS_MB, self_back)
            def tile(cols, start):
                tmp[0:DEC_MB, cols] = dot_nt(qkv[rows, :], wa[cols_at(start, DEEP), 0 : 3 * D])

            tiles(DEEP, tile)

            def low_back(i):
                part = rows_at(base + i * ROW, ROW)
                grad, gain_row = norm_back(
                    tmp[rows_at(i * ROW, ROW), :], x[part, :].astype(WIDE), first_gain
                )
                x1[part, :] = x1[part, :] + grad
                exch[rows_at(DEC_ROWS + base + i * ROW, ROW), :] = x1[part, 0:HALF].astype(LOW)
                add_gain(0, gain_row)

            loop(ROWS_MB, low_back)
            for half, kept in enumerate((exch, decoded_half)):
                cols = slice(half * HALF, (half + 1) * HALF)
                kept[rows, :] = (x2[rows, cols] + dot_nn(u[rows, :], wo[:, cols])).astype(LOW)

        loop(MICRO, finish)
        late = [
            store(qkv.at[full], dqkv_out.at[full], 4), store(g1.at[full], g1_out.at[full], 5),
            store(x1.at[full, HALF:], caption_own, 8), store(exch, exch_out, 9),
            store(decoded_half, decoded_own, 15),
        ]
        for copy in late:
            copy.start()
        for copy in stores + late:
            copy.wait()
        for micro in range(MICRO):
            across(sent.at[micro], micro).wait_send()
        ctx_copy(ctx_part(quarter), quarter, {"dp": side}, 1).wait_send()
        ctx_copy(ctx_part(quarter), quarter, {"dp": twin}, 2).wait_send()
        ctx_copy(ctx_part(quarter), quarter, {"dp": twin}, 3).wait_send()

    gain_in.wait()
    first_gain, second_gain, third_gain = gain_rows[0:1, :], gain_rows[1:2, :], gain_rows[2:3, :]

    @pl.when(section == 0)
    def _():
        encoder()

    @pl.when(section == 1)
    def _():
        decoder()


def main_call(patches, captions, segments, seg_images, attn_w, w_in, w_out, gains, cot):
    def low(*shape):
        return jax.ShapeDtypeStruct(shape, LOW)

    def wide(*shape):
        return jax.ShapeDtypeStruct(shape, WIDE)

    outs = [
        low(ENC_ROWS, D), low(ENC_ROWS, D), low(DEC_ROWS, D), low(ENC_ROWS, D), low(ENC_ROWS, FF),
        low(ENC_ROWS, 3 * D), low(ENC_ROWS, D), low(ENC_ROWS, D), low(ENC_ROWS, FF),
        low(DEC_ROWS, D), low(DEC_ROWS, D), low(MICRO, ENC_MB, D), low(ENC_ROWS, 2 * D),
        wide(8, D), wide(ENC_ROWS, HALF), low(DEC_ROWS, HALF), wide(DEC_ROWS, HALF),
        low(2 * DEC_ROWS, HALF),
    ]
    any_spec = pl.BlockSpec(memory_space=pl.ANY)
    vmem_spec = pl.BlockSpec(memory_space=pltpu.VMEM)
    out_specs = [any_spec] * len(outs)
    out_specs[13] = vmem_spec
    vmem = pltpu.VMEM
    scratch = [
        vmem((D, 6 * D), LOW), vmem((D, FF), LOW), vmem((FF, D), LOW), vmem((D, 2 * D), LOW),
        vmem((ENC_ROWS, D), LOW), vmem((DEC_ROWS, D), LOW),
        vmem((ENC_ROWS, D), LOW), vmem((ENC_ROWS, D), LOW), vmem((ENC_ROWS, D), LOW),
        vmem((ENC_ROWS, D), LOW),
        vmem((ENC_ROWS, 3 * D), LOW), vmem((max(ENC_MB, DEC_ROWS), FF), LOW), vmem((ENC_ROWS, FF), LOW),
        vmem((ENC_ROWS, D), WIDE), vmem((ENC_ROWS, D), WIDE),
        vmem((ENC_ROWS, D), LOW), vmem((ENC_ROWS, D), LOW),
        vmem((MICRO, ENC_MB, D), LOW), vmem((max(ENC_MB, DEC_ROWS), D), LOW),
        vmem((ENC_ROWS, 2 * D), LOW),
        vmem((DEC_ROWS, D), LOW), vmem((DEC_ROWS, D), LOW), vmem((DEC_ROWS, D), WIDE),
        vmem((ENC_MB, D), WIDE), vmem((MICRO, ENC_MB, D), LOW),
        vmem((DEC_MB, ENC_MB), WIDE), vmem((ROWS_MB, ENC_MB, ROW), WIDE),
        vmem((2 * DEC_ROWS, HALF), LOW), vmem((DEC_ROWS, HALF), LOW),
        vmem((3, D), WIDE), pltpu.SemaphoreType.DMA((7,)), pltpu.SemaphoreType.DMA((16,)),
        pltpu.SemaphoreType.DMA((MICRO,)), pltpu.SemaphoreType.DMA((MICRO,)),
        pltpu.SemaphoreType.DMA((4,)), pltpu.SemaphoreType.DMA((4,)),
    ]
    return pl.pallas_call(
        main_kernel,
        name="layers",
        out_shape=outs,
        in_specs=[any_spec, any_spec, vmem_spec, pl.BlockSpec(memory_space=pltpu.SMEM)]
        + [any_spec] * 5,
        out_specs=out_specs,
        scratch_shapes=scratch,
        compiler_params=pltpu.CompilerParams(
            collective_id=1, has_side_effects=True, vmem_limit_bytes=63 * MIB
        ),
    )(patches, captions, segments, seg_images, attn_w, w_in, w_out, gains, cot)


CHUNK = 256
SLOTS = 8
FIRST_LAG = 2
FAR_EVERY = 6
LAG = 4
GAIN_STEPS = 5
OUT_IDS = 12
ONLY_DEC = 12
CTX_IDS = 6


def grads_kernel(n_bits, *refs):
    (
        a_in, o_in, c_in, b_in, u_in, dqkv_in, g1_in, g2_in, dh_in, co_in, dq_in, up_in, dctx_in,
        gains_in, patch_own, decoded_own, caption_own, exch_in, cot_in,
        shares, gain_share, patch_out, decoded_out, caption_out,
        a, o, c, b, u, dqkv, g1, g2, dh, co, dq, up, dctx, cot,
        part, ctx_sum, exch, patch_rows, gain_sum, gain_in,
    ) = refs[:44]
    recv = refs[44 : 44 + n_bits]
    load_sem, own_sem, send_sem, recv_sem, gain_send, gain_recv, far_send, far_recv = refs[44 + n_bits :]
    section = lax.axis_index("section")
    dp = lax.axis_index("dp")
    bits = [(dp // (1 << k)) % 2 for k in range(n_bits)]
    partners = [{"dp": dp + (1 << k) * (1 - 2 * bits[k])} for k in range(n_bits)]
    across = {"section": 1 - section}
    barrier = pltpu.get_barrier_semaphore()

    def greet(target):
        pl.semaphore_signal(barrier, inc=1, device_id=target, device_id_type=MESH)

    for target in partners:
        greet(target)

    @pl.when(section == 1)
    def _():
        pl.semaphore_wait(barrier, n_bits)
        greet(across)

    @pl.when(section == 0)
    def _():
        pl.semaphore_wait(barrier, n_bits + 1)
        greet(across)

    rows = part.shape[-2]
    owners = 1 << n_bits
    total = recv[0].shape[0]
    begin = ONLY_DEC * (1 - section)

    def remote(src, dst, send, receive, target):
        return pltpu.make_async_remote_copy(
            src_ref=src, dst_ref=dst, send_sem=send, recv_sem=receive, device_id=target,
            device_id_type=MESH)

    def gain_copy(k):
        return remote(gain_sum.at[k], gain_in.at[k], gain_send.at[k], gain_recv.at[k], partners[k])

    def exch_copy():
        return remote(exch_in, exch, far_send.at[0], far_recv.at[0], across)

    def ctx_copy():
        return remote(ctx_sum, shares.at[0:CTX_IDS], far_send.at[1], far_recv.at[1], across)

    gain_sum[0] = gains_in[...]
    gain_copy(0).start()

    def load_plan(is_dec):
        count = DEC_ROWS if is_dec else ENC_ROWS

        def short(src, dst):
            return src.at[0:count], dst.at[0:count]

        plan = {
            0: short(u_in, u), 1: short(g2_in, g2), 2: short(b_in, b), 3: short(dh_in, dh),
            4: short(a_in, a), 5: short(dqkv_in, dqkv), 6: short(o_in, o), 7: short(g1_in, g1),
        }
        if is_dec:
            only = {
                8: (up_in, up), 9: (dctx_in, dctx), 10: (c_in, c), 11: (dq_in, dq),
                12: (co_in, co), 13: (cot_in, cot),
            }
            plan = {**only, **plan}
        return plan

    def need(is_dec, *slots):
        plan = load_plan(is_dec)
        for slot in slots:
            pltpu.make_async_copy(*plan[slot], load_sem.at[slot]).wait()

    for is_dec in (False, True):
        @pl.when(section == int(is_dec))
        def _(is_dec=is_dec):
            for slot, (src, dst) in load_plan(is_dec).items():
                pltpu.make_async_copy(src, dst, load_sem.at[slot]).start()
            if is_dec:
                pltpu.make_async_copy(decoded_own, decoded_out, load_sem.at[14]).start()
                pltpu.make_async_copy(caption_own, caption_out, load_sem.at[15]).start()
            else:
                pltpu.make_async_copy(patch_own, patch_rows, load_sem.at[14]).start()

    def core_copy(index):
        slot = index % SLOTS
        return remote(part.at[slot, 1 - bits[0]], recv[0].at[index], send_sem.at[0, index],
                      recv_sem.at[0, index], partners[0])

    near_first = list(range(1, n_bits))
    far_first = list(range(2, n_bits)) + [1]

    def stage_cut(order, stage, index, flip):
        bit = order[stage - 1]
        left = sorted(order[stage - 1 :], reverse=True)
        value = bits[bit] + flip * (1 - 2 * bits[bit])
        return (index,) + (slice(None),) * left.index(bit) + (value,)

    def stage_copy(order, stage, index):
        return remote(
            recv[stage - 1].at[stage_cut(order, stage, index, 1)], recv[stage].at[index],
            send_sem.at[stage, index], recv_sem.at[stage, index], partners[order[stage - 1]])

    def in_order(index, action):
        is_far = index % FAR_EVERY == FAR_EVERY // 2

        @pl.when(is_far)
        def _():
            action(far_first)

        @pl.when(jnp.logical_not(is_far))
        def _():
            action(near_first)

    def advance(i):
        for stage in range(n_bits):
            j = i - FIRST_LAG - stage * LAG

            @pl.when((j >= begin) & (j < total))
            def _(stage=stage, j=j):
                if stage == 0:
                    core_copy(j).wait()
                    summed = part[j % SLOTS, bits[0]].astype(WIDE) + recv[0][j].astype(WIDE)
                    recv[0][j] = summed.astype(LOW)
                    in_order(j, lambda order: stage_copy(order, 1, j).start())
                elif stage < n_bits - 1:
                    def step(order):
                        stage_copy(order, stage, j).wait()
                        mine = recv[stage - 1][stage_cut(order, stage, j, 0)]
                        summed = mine.astype(WIDE) + recv[stage][j].astype(WIDE)
                        recv[stage][j] = summed.astype(LOW)
                        stage_copy(order, stage + 1, j).start()

                    in_order(j, step)
                else:
                    def step(order):
                        stage_copy(order, stage, j).wait()

                    in_order(j, step)
                    last = jnp.where(j % FAR_EVERY == FAR_EVERY // 2, bits[far_first[-1]], bits[near_first[-1]])
                    mine = recv[stage - 1][j, last]
                    summed = mine.astype(WIDE) + recv[stage][j].astype(WIDE)

                    @pl.when(j < CTX_IDS)
                    def _():
                        ctx_sum[j] = summed

                    @pl.when(j >= CTX_IDS)
                    def _():
                        shares[j - CTX_IDS] = summed

        for k in range(n_bits):
            @pl.when(i == ONLY_DEC + GAIN_STEPS * (k + 1))
            def _(k=k):
                gain_copy(k).wait()
                summed = gain_sum[k] + gain_in[k]
                if k == n_bits - 1:
                    own = jnp.zeros((8, rows), WIDE)
                    for owner in range(owners):
                        own = jnp.where(dp == owner, summed[:, owner * rows : (owner + 1) * rows], own)
                    gain_share[...] = own
                else:
                    gain_sum[k + 1] = summed
                    gain_copy(k + 1).start()

    def place(index, first_owner, block):
        for k in range(block.shape[0] // rows):
            owner = first_owner + k
            path = tuple((owner >> bit) & 1 for bit in reversed(range(1, n_bits)))
            part[(index % SLOTS, owner & 1) + path] = block[k * rows : (k + 1) * rows].astype(LOW)

    def simple_phase(first, count, left, right, col, row_count):
        def step(i):
            index = first + i
            cols = cols_at(col + i * CHUNK, CHUNK)
            if row_count is None:
                value = dot_tn(left[...].reshape(-1, D), right[:, cols])
            else:
                value = dot_tn(left[0:row_count, :], right[0:row_count, cols])
            place(index, 0, value)
            core_copy(index).start()
            advance(index)
        loop(count, step)

    def out_phase(first, right, row_count):
        share = FF // owners
        blocks = share // rows
        step_owners = D // share

        def step(i):
            cols = cols_at(i * CHUNK, CHUNK)
            base = first + i * blocks
            for piece in range(FF // D):
                value = dot_tn(u[0:row_count, piece * D : (piece + 1) * D], right[0:row_count, cols])
                for k in range(step_owners):
                    for q in range(blocks):
                        low = k * share + q * rows
                        place(base + q, piece * step_owners + k, value[low : low + rows])
            loop(blocks, lambda q: core_copy(base + q).start())
            loop(blocks, lambda q: advance(base + q))
        loop(D // CHUNK, step)

    @pl.when(section == 1)
    def _():
        need(True, 8, 9)
        simple_phase(0, CTX_IDS, up, dctx, 0, None)
        need(True, 10, 11)
        simple_phase(CTX_IDS, 3, c, dq, 0, DEC_ROWS)
        need(True, 12, 1)
        simple_phase(CTX_IDS + 3, 3, co, g2, 0, DEC_ROWS)

    for is_dec in (False, True):
        @pl.when(section == int(is_dec))
        def _(is_dec=is_dec):
            count = DEC_ROWS if is_dec else ENC_ROWS
            need(is_dec, 0, 13 if is_dec else 1)
            out_phase(ONLY_DEC, cot if is_dec else g2, count)
            need(is_dec, 2, 3)
            simple_phase(ONLY_DEC + OUT_IDS, FF // CHUNK, b, dh, 0, count)

    @pl.when(section == 1)
    def _():
        pl.semaphore_wait(barrier, 1)
        ctx_copy().start()

    exch_copy().start()

    for is_dec in (False, True):
        @pl.when(section == int(is_dec))
        def _(is_dec=is_dec):
            count = DEC_ROWS if is_dec else ENC_ROWS
            need(is_dec, 4, 5)
            first = ONLY_DEC + OUT_IDS + FF // CHUNK
            simple_phase(first, 3 * D // CHUNK, a, dqkv, 0, count)
            need(is_dec, 6, 7)
            simple_phase(first + 3 * D // CHUNK, D // CHUNK, o, g1, 0, count)

    exch_copy().wait()

    @pl.when(section == 0)
    def _():
        pltpu.make_async_copy(patch_own, patch_rows, load_sem.at[14]).wait()
        for image in range(MICRO * IMG_MB):
            patch_out[image * PATCHES : (image + 1) * PATCHES, :] = patch_rows[
                image * IMG_ROWS : image * IMG_ROWS + PATCHES, :
            ]
        decoded_out[...] = exch[0:DEC_ROWS, :]
        caption_out[...] = exch[DEC_ROWS : 2 * DEC_ROWS, :].astype(WIDE)

    @pl.when(section == 1)
    def _():
        pltpu.make_async_copy(decoded_own, decoded_out, load_sem.at[14]).wait()
        pltpu.make_async_copy(caption_own, caption_out, load_sem.at[15]).wait()
        for image in range(MICRO * IMG_MB):
            patch_out[image * PATCHES : (image + 1) * PATCHES, :] = exch[
                image * IMG_ROWS : image * IMG_ROWS + PATCHES, :
            ].astype(WIDE)

    loop(FIRST_LAG + (n_bits - 1) * LAG, lambda i: advance(total + i))

    @pl.when(section == 0)
    def _():
        ctx_copy().wait_recv()

    @pl.when(section == 1)
    def _():
        ctx_copy().wait_send()


def grads_call(n_dp, *operands):
    n_bits = n_dp.bit_length() - 1
    rows = D // n_dp
    share = FF // n_dp
    total = ONLY_DEC + 2 * OUT_IDS + 4 * D // CHUNK
    vmem = pltpu.VMEM
    pair = (2,) * (n_bits - 1)
    any_spec = pl.BlockSpec(memory_space=pl.ANY)
    vmem_spec = pl.BlockSpec(memory_space=pltpu.VMEM)
    sem = pltpu.SemaphoreType.DMA
    scratch = [
        vmem((ENC_ROWS, D), LOW), vmem((ENC_ROWS, D), LOW), vmem((DEC_ROWS, D), LOW),
        vmem((ENC_ROWS, D), LOW), vmem((ENC_ROWS, FF), LOW), vmem((ENC_ROWS, 3 * D), LOW),
        vmem((ENC_ROWS, D), LOW), vmem((ENC_ROWS, D), LOW), vmem((ENC_ROWS, FF), LOW),
        vmem((DEC_ROWS, D), LOW), vmem((DEC_ROWS, D), LOW), vmem((MICRO, ENC_MB, D), LOW),
        vmem((ENC_ROWS, 2 * D), LOW), vmem((DEC_ROWS, D), LOW),
        vmem((SLOTS, 2) + pair + (rows, CHUNK), LOW), vmem((CTX_IDS, rows, CHUNK), WIDE),
        vmem((2 * DEC_ROWS, HALF), LOW), vmem((ENC_ROWS, HALF), WIDE),
        vmem((n_bits, 8, D), WIDE), vmem((n_bits, 8, D), WIDE),
    ]
    scratch += [vmem((total,) + pair[k:] + (rows, CHUNK), LOW) for k in range(n_bits)]
    scratch += [
        sem((16,)), sem((1,)), sem((n_bits, total)), sem((n_bits, total)), sem((n_bits,)),
        sem((n_bits,)), sem((2,)), sem((2,)),
    ]
    in_specs = [any_spec] * len(operands)
    in_specs[13] = vmem_spec
    return pl.pallas_call(
        functools.partial(grads_kernel, n_bits),
        name="weight_sums",
        out_shape=(
            jax.ShapeDtypeStruct((total - CTX_IDS, rows, CHUNK), WIDE),
            jax.ShapeDtypeStruct((8, rows), WIDE),
            jax.ShapeDtypeStruct((MICRO * IMG_MB * PATCHES, HALF), WIDE),
            jax.ShapeDtypeStruct((DEC_ROWS, HALF), LOW),
            jax.ShapeDtypeStruct((DEC_ROWS, HALF), WIDE),
        ),
        in_specs=in_specs,
        out_specs=(vmem_spec,) * 5,
        scratch_shapes=scratch,
        compiler_params=pltpu.CompilerParams(
            collective_id=2, has_side_effects=True, vmem_limit_bytes=63 * MIB
        ),
    )(*operands)


def place_kernel(
    shares, gain_share, patch_in, decoded_in, caption_in,
    decoded_out, caption_out, patch_out, attn_out, in_out, out_out, gain_out, sem,
):
    rows = shares.shape[1]
    moves = [
        (patch_in, patch_out), (caption_in, caption_out), (decoded_in, decoded_out),
        (gain_share.at[0:3], gain_out.at[0]),
    ]
    first_w_in = CTX_IDS + OUT_IDS
    first_attn = first_w_in + FF // CHUNK
    blocks = OUT_IDS * CHUNK // D

    def cols(index):
        return slice(index * CHUNK, (index + 1) * CHUNK)

    for k in range(4 * D // CHUNK):
        moves.append((shares.at[first_attn + k], attn_out.at[0, :, cols(k)]))
    for k in range(CTX_IDS):
        moves.append((shares.at[k], attn_out.at[0, :, cols(4 * D // CHUNK + k)]))
    for k in range(FF // CHUNK):
        moves.append((shares.at[first_w_in + k], in_out.at[0, :, cols(k)]))
    for k in range(OUT_IDS):
        part = slice((k % blocks) * rows, (k % blocks + 1) * rows)
        moves.append((shares.at[CTX_IDS + k], out_out.at[0, part, cols(k // blocks)]))
    copies = [
        pltpu.make_async_copy(src, dst, sem.at[index]) for index, (src, dst) in enumerate(moves)
    ]
    for copy in copies:
        copy.start()
    for copy in copies:
        copy.wait()


def kernel_sums(n_dp, operands):
    results = grads_call(n_dp, *operands)
    rows = D // n_dp
    any_spec = pl.BlockSpec(memory_space=pl.ANY)
    patch_out, decoded_out, caption_out = results[2:]
    shapes = [decoded_out, caption_out, patch_out] + [
        jax.ShapeDtypeStruct(shape, WIDE)
        for shape in ((1, rows, 6 * D), (1, rows, FF), (1, FF // n_dp, D), (1, 3, rows))
    ]
    return pl.pallas_call(
        place_kernel,
        name="place_sums",
        out_shape=[jax.ShapeDtypeStruct(item.shape, item.dtype) for item in shapes],
        in_specs=[any_spec] * 5,
        out_specs=[pl.BlockSpec(memory_space=pltpu.VMEM)] * 7,
        scratch_shapes=[pltpu.SemaphoreType.DMA((64,))],
    )(*results)


def shifted(block, distance):
    devices = range(lax.axis_size("section"))
    route = [(i - distance, i) for i in devices if i - distance in devices]
    return lax.ppermute(block, "section", route)


def plain_sums(operands):
    (
        a, o, c, b, u, dqkv, g1, g2, dh, co, dq, up, dctx,
        gains, patch_own, decoded_own, caption_own, exch, cot,
    ) = operands
    is_first = lax.axis_index("section") == 0
    up = up.reshape(ENC_ROWS, D)

    def encoder_parts():
        return (
            jnp.concatenate([dot_tn(a, dqkv), dot_tn(o, g1)], 1), jnp.zeros((D, 2 * D), WIDE),
            jnp.zeros((D, 2 * D), WIDE), dot_tn(b, dh), dot_tn(u, g2),
        )

    def decoder_parts():
        rows = slice(0, DEC_ROWS)
        return (
            jnp.concatenate([dot_tn(a[rows], dqkv[rows]), dot_tn(o[rows], g1[rows])], 1),
            jnp.concatenate([dot_tn(c, dq), dot_tn(co, g2[rows])], 1),
            dot_tn(up, dctx), dot_tn(b[rows], dh[rows]), dot_tn(u[rows], cot),
        )

    parts = lax.cond(is_first, encoder_parts, decoder_parts)
    sums = [lax.psum_scatter(part, "dp", scatter_dimension=0, tiled=True) for part in parts]
    last = jnp.where(is_first, shifted(sums[2], -1), sums[1])
    moved = lax.ppermute(exch, "section", [(0, 1), (1, 0)])

    def unpad(block):
        shaped = block[:ENC_ROWS].reshape(MICRO * IMG_MB, IMG_ROWS, HALF)
        return shaped[:, :PATCHES].reshape(-1, HALF).astype(WIDE)

    return (
        jnp.where(is_first, moved[:DEC_ROWS], decoded_own),
        jnp.where(is_first, moved[DEC_ROWS:].astype(WIDE), caption_own),
        jnp.where(is_first, unpad(patch_own), unpad(moved)),
        jnp.concatenate([sums[0], last], 1),
        sums[3],
        sums[4],
        lax.psum_scatter(gains[:3], "dp", scatter_dimension=1, tiled=True),
    )


def with_section(results):
    return tuple(results[:3]) + tuple(share[None] for share in results[3:])


def local(patches, captions, segments, seg_images, attn_w, w_in, w_out, norm_gains, cotangent):
    n_dp = lax.axis_size("dp")
    kept = main_call(
        patches, captions, segments, seg_images, attn_w, w_in, w_out, norm_gains, cotangent
    )
    operands = list(kept) + [cotangent]
    if n_dp & (n_dp - 1) == 0 and (D // n_dp) % 16 == 0:
        results = kernel_sums(n_dp, operands)
    else:
        results = with_section(plain_sums(operands))
    return tuple(results)


def solution(mesh):
    placed = (
        P("dp", None),
        P("dp", None),
        P("dp", None),
        P("dp", None),
        P("section", None, None),
        P("section", None, None),
        P("section", None, None),
        P("section", None, None),
        P("dp", None),
    )
    return jax.shard_map(
        local,
        mesh=mesh,
        in_specs=placed,
        out_specs=(
            P("dp", "section"),
            P("dp", "section"),
            P("dp", "section"),
            P("section", "dp", None),
            P("section", "dp", None),
            P("section", "dp", None),
            P("section", None, "dp"),
        ),
        check_vma=False,
    )
```

profile of v0, /device:TPU:0, one launch (start us, length us, event | category | flops | bytes accessed | tf_op | source)
XLA Modules:
  0.0 212.8 jit_solution(17600008593193701835)
XLA Ops:
  0.6 1.3 copy.16.refs_7_
  1.9 110.7 %layers.1 = (bf16[832,768]{1,0:T(8,128)(2,1)}, bf16[832,768]{1,0:T(8,128)(2,1)}, bf16[512,768]{1,0:T(8,128)(2,1)}, bf16[832,768]{1,0:T(8,128)(2,1)}, bf16[832,30...) custom-call(bf16[784,768]{1,0:T(8,128)(2,1)} %refs_0_.1, ...), custom_call_target="tpu_custom_call" | custom-call | tf_op jit(solution)/shard_map/layers/pallas_call | solution.py:760
  112.7 94.0 %weight_sums.1 = (f32[42,48,256]{2,1,0:T(8,128)}, f32[8,48]{1,0:T(8,128)}, f32[784,384]{1,0:T(8,128)}, bf16[512,384]{1,0:T(8,128)(2,1)}, f32[512,384]{1,0:T(8,128)}) custom-call(bf16[832,768]{1,0:T(8,128)(2,1)} %get-tuple-element.30.refs_0_, bf16[832,768]{1,0:T(8,128)(2,1)} %get-tuple-element.31.refs_1_, bf16[512,768]{1,0:T(8,128)(2,1)} %get-tuple-element.32.refs_2_, ...), custom_call_target="tpu_custom_call" | custom-call | tf_op jit(solution)/shard_map/weight_sums/pallas_call | solution.py:1086
  206.7 4.9 %place_sums.1 = (bf16[512,384]{1,0:T(8,128)(2,1)}, f32[512,384]{1,0:T(8,128)}, f32[784,384]{1,0:T(8,128)}, f32[1,48,4608]{2,1,0:T(8,128)}, f32[1,48,3072]{2,1,0:...) custom-call(f32[42,48,256]{2,1,0:T(8,128)} %get-tuple-element.48.shares, f32[8,48]{1,0:T(8,128)} %get-tuple-element.49.gain_share, ...), custom_call_target="tpu_custom_call" | custom-call | tf_op jit(solution)/shard_map/place_sums/pallas_call | solution.py:1148
  211.6 1.2 copy.17
where the time goes:
time: 214 us; the launch traced here: 213 us
  Pallas kernels  210 us (98%)
  local copies, waits for them, and re-layouts  2.5 us (1%)
    pallas_call x1, Pallas kernels, main_call(): pl.pallas_call(main_kernel, name='layers', out_shape=outs, in_specs=[any_...  111 us
    pallas_call x1, Pallas kernels, grads_call(): pl.pallas_call(functools.partial(grads_kernel, n_bits), name='weight_sums...  94 us
    pallas_call x1, Pallas kernels, kernel_sums(): pl.pallas_call(place_kernel, name='place_sums', out_shape=[jax.ShapeDtype...  4.88 us

commit v1 on v0

--- a/solution.py
+++ b/solution.py
@@ -774,6 +774,8 @@
 CHUNK = 256
 SLOTS = 8
 FIRST_LAG = 2
+FIRST_ENC = (6, 7, 0, 1)
+FIRST_DEC = (8, 9, 10, 11)
 FAR_EVERY = 6
 LAG = 4
 GAIN_STEPS = 5
@@ -860,16 +862,23 @@
         for slot in slots:
             pltpu.make_async_copy(*plan[slot], load_sem.at[slot]).wait()
 
+    def fetch(is_dec, *slots):
+        plan = load_plan(is_dec)
+        for slot in slots:
+            pltpu.make_async_copy(*plan[slot], load_sem.at[slot]).start()
+
+    def fetch_rest(is_dec):
+        fetch(is_dec, *[k for k in load_plan(is_dec) if k not in (FIRST_DEC if is_dec else FIRST_ENC)])
+        if is_dec:
+            pltpu.make_async_copy(decoded_own, decoded_out, load_sem.at[14]).start()
+            pltpu.make_async_copy(caption_own, caption_out, load_sem.at[15]).start()
+        else:
+            pltpu.make_async_copy(patch_own, patch_rows, load_sem.at[14]).start()
+
     for is_dec in (False, True):
         @pl.when(section == int(is_dec))
         def _(is_dec=is_dec):
-            for slot, (src, dst) in load_plan(is_dec).items():
-                pltpu.make_async_copy(src, dst, load_sem.at[slot]).start()
-            if is_dec:
-                pltpu.make_async_copy(decoded_own, decoded_out, load_sem.at[14]).start()
-                pltpu.make_async_copy(caption_own, caption_out, load_sem.at[15]).start()
-            else:
-                pltpu.make_async_copy(patch_own, patch_rows, load_sem.at[14]).start()
+            fetch(is_dec, *(FIRST_DEC if is_dec else FIRST_ENC))
 
     def core_copy(index):
         slot = index % SLOTS
@@ -992,6 +1001,7 @@
     @pl.when(section == 1)
     def _():
         need(True, 8, 9)
+        fetch_rest(True)
         simple_phase(0, CTX_IDS, up, dctx, 0, None)
         need(True, 10, 11)
         simple_phase(CTX_IDS, 3, c, dq, 0, DEC_ROWS)
@@ -1002,10 +1012,14 @@
         @pl.when(section == int(is_dec))
         def _(is_dec=is_dec):
             count = DEC_ROWS if is_dec else ENC_ROWS
+            need(is_dec, 6, 7)
+            if not is_dec:
+                fetch_rest(False)
+            simple_phase(ONLY_DEC, D // CHUNK, o, g1, 0, count)
             need(is_dec, 0, 13 if is_dec else 1)
-            out_phase(ONLY_DEC, cot if is_dec else g2, count)
+            out_phase(ONLY_DEC + D // CHUNK, cot if is_dec else g2, count)
             need(is_dec, 2, 3)
-            simple_phase(ONLY_DEC + OUT_IDS, FF // CHUNK, b, dh, 0, count)
+            simple_phase(ONLY_DEC + D // CHUNK + OUT_IDS, FF // CHUNK, b, dh, 0, count)
 
     @pl.when(section == 1)
     def _():
@@ -1019,10 +1033,8 @@
         def _(is_dec=is_dec):
             count = DEC_ROWS if is_dec else ENC_ROWS
             need(is_dec, 4, 5)
-            first = ONLY_DEC + OUT_IDS + FF // CHUNK
+            first = ONLY_DEC + D // CHUNK + OUT_IDS + FF // CHUNK
             simple_phase(first, 3 * D // CHUNK, a, dqkv, 0, count)
-            need(is_dec, 6, 7)
-            simple_phase(first + 3 * D // CHUNK, D // CHUNK, o, g1, 0, count)
 
     exch_copy().wait()
 
@@ -1111,22 +1123,26 @@
         (patch_in, patch_out), (caption_in, caption_out), (decoded_in, decoded_out),
         (gain_share.at[0:3], gain_out.at[0]),
     ]
-    first_w_in = CTX_IDS + OUT_IDS
+    mixed_ids = D // CHUNK
+    first_w_out = CTX_IDS + mixed_ids
+    first_w_in = first_w_out + OUT_IDS
     first_attn = first_w_in + FF // CHUNK
     blocks = OUT_IDS * CHUNK // D
 
     def cols(index):
         return slice(index * CHUNK, (index + 1) * CHUNK)
 
-    for k in range(4 * D // CHUNK):
+    for k in range(3 * mixed_ids):
         moves.append((shares.at[first_attn + k], attn_out.at[0, :, cols(k)]))
+    for k in range(mixed_ids):
+        moves.append((shares.at[CTX_IDS + k], attn_out.at[0, :, cols(3 * mixed_ids + k)]))
     for k in range(CTX_IDS):
         moves.append((shares.at[k], attn_out.at[0, :, cols(4 * D // CHUNK + k)]))
     for k in range(FF // CHUNK):
         moves.append((shares.at[first_w_in + k], in_out.at[0, :, cols(k)]))
     for k in range(OUT_IDS):
         part = slice((k % blocks) * rows, (k % blocks + 1) * rows)
-        moves.append((shares.at[CTX_IDS + k], out_out.at[0, part, cols(k // blocks)]))
+        moves.append((shares.at[first_w_out + k], out_out.at[0, part, cols(k // blocks)]))
     copies = [
         pltpu.make_async_copy(src, dst, sem.at[index]) for index, (src, dst) in enumerate(moves)
     ]

time: 214 us -> 220 us (1.028)
  Pallas kernels: 210 us -> 216 us
    pallas_call x1, Pallas kernels: 94 us -> 100 us  [grads_call(): pl.pallas_call(functools.partial(grads_kernel, n_bits), name='weight_sums...]
where the time goes in v1:
time: 220 us; the launch traced here: 219 us
  Pallas kernels  216 us (98%)
  local copies, waits for them, and re-layouts  2.5 us (1%)
    pallas_call x1, Pallas kernels, main_call(): pl.pallas_call(main_kernel, name='layers', out_shape=outs, in_specs=[any_...  111 us
    pallas_call x1, Pallas kernels, grads_call(): pl.pallas_call(functools.partial(grads_kernel, n_bits), name='weight_sums...  100 us
    pallas_call x1, Pallas kernels, kernel_sums(): pl.pallas_call(place_kernel, name='place_sums', out_shape=[jax.ShapeDtype...  4.88 us

profile of v1, /device:TPU:0, one launch (start us, length us, event | category | flops | bytes accessed | tf_op | source)
XLA Modules:
  0.0 219.3 jit_solution(17271626784035241574)
XLA Ops:
  0.6 1.3 copy.16.refs_7_
  1.9 110.7 %layers.1 = (bf16[832,768]{1,0:T(8,128)(2,1)}, bf16[832,768]{1,0:T(8,128)(2,1)}, bf16[512,768]{1,0:T(8,128)(2,1)}, bf16[832,768]{1,0:T(8,128)(2,1)}, bf16[832,30...) custom-call(bf16[784,768]{1,0:T(8,128)(2,1)} %refs_0_.1, ...), custom_call_target="tpu_custom_call" | custom-call | tf_op jit(solution)/shard_map/layers/pallas_call | solution.py:760
  112.7 100.5 %weight_sums.1 = (f32[42,48,256]{2,1,0:T(8,128)}, f32[8,48]{1,0:T(8,128)}, f32[784,384]{1,0:T(8,128)}, bf16[512,384]{1,0:T(8,128)(2,1)}, f32[512,384]{1,0:T(8,128)}) custom-call(bf16[832,768]{1,0:T(8,128)(2,1)} %get-tuple-element.30.refs_0_, bf16[832,768]{1,0:T(8,128)(2,1)} %get-tuple-element.31.refs_1_, bf16[512,768]{1,0:T(8,128)(2,1)} %get-tuple-element.32.refs_2_, ...), custom_call_target="tpu_custom_call" | custom-call | tf_op jit(solution)/shard_map/weight_sums/pallas_call | solution.py:1098
  213.2 4.9 %place_sums.1 = (bf16[512,384]{1,0:T(8,128)(2,1)}, f32[512,384]{1,0:T(8,128)}, f32[784,384]{1,0:T(8,128)}, f32[1,48,4608]{2,1,0:T(8,128)}, f32[1,48,3072]{2,1,0:...) custom-call(f32[42,48,256]{2,1,0:T(8,128)} %get-tuple-element.48.shares, f32[8,48]{1,0:T(8,128)} %get-tuple-element.49.gain_share, ...), custom_call_target="tpu_custom_call" | custom-call | tf_op jit(solution)/shard_map/place_sums/pallas_call | solution.py:1164
  218.1 1.2 copy.17
